TPU v7x, 128 devices: a whole 4x4x4 slice. The times are simulated.
128 devices in a mesh: replica: 16 (over z_hi, x, core), shard: 8 (over z_lo, y).
Axes of the slice: x: 4, y: 4, z: 4 (z_hi: 2, z_lo: 2; z = z_hi * 2 + z_lo), core: 2. Of those that a mesh axis runs over, the one named last changes fastest.
Arguments:
- gate_pre: bfloat16 [16384, 3584], P(('replica', 'shard')), may hold values from -6 to 6
- up_pre: bfloat16 [16384, 3584], P(('replica', 'shard')), may hold values from -6 to 6
- out_grad: bfloat16 [16384, 8192], P(('replica', 'shard')), may hold values from -24 to 24
- w_down: bfloat16 [8192, 3584], P(None, 'shard'), may hold values from -0.0625 to 0.0625
- m_down: float32 [8192, 3584], P('replica', 'shard'), may hold values from -3 to 3
- v_down: float32 [8192, 3584], P('replica', 'shard'), may hold values from 0.02 to 0.5
Outputs:
- d_gate_up: bfloat16 [16384, 2, 3584], P(('replica', 'shard'))
- direction_down: bfloat16 [8192, 3584], P(None, 'shard')
- first_down: float32 [8192, 3584], P('replica', 'shard')
- second_down: float32 [8192, 3584], P('replica', 'shard')
All inputs are finite; a program needn't handle non-finite values.
Results may differ from a plain program's by a relative error of at most 0.005.
Values may be sent and summed in bfloat16 or wider, within the bound.
A program may use at most 128 MiB of HBM per device.

v0:
```python
import math

import jax
import jax.numpy as jnp
from jax import lax
from jax.sharding import PartitionSpec as P

beta_one = 0.9
beta_two = 0.95
epsilon = 1e-08
bias_one = 1.0 - beta_one**10
bias_two = 1.0 - beta_two**10


def local_grads(gate, up, d_hidden):
    sig = jax.nn.sigmoid(gate)
    active = gate * sig
    hidden = (active * up).astype(jnp.bfloat16)
    d_gate = d_hidden * up * sig * (1.0 + gate * (1.0 - sig))
    d_up = d_hidden * active
    return (hidden, jnp.stack([d_gate, d_up], axis=1).astype(jnp.bfloat16))


def contract_rows(left, right):
    return lax.dot_general(
        left, right, (((0,), (0,)), ((), ())), preferred_element_type=jnp.float32
    )


def adam_step(first, second, grad):
    first_new = beta_one * first + (1.0 - beta_one) * grad
    second_new = beta_two * second + (1.0 - beta_two) * grad * grad
    direction = first_new / bias_one / (jnp.sqrt(second_new / bias_two) + epsilon)
    return (direction.astype(jnp.bfloat16), first_new, second_new)


def local(gate_pre, up_pre, out_grad, w_down, m_down, v_down):
    total_tokens = gate_pre.shape[0] * lax.axis_size("replica") * lax.axis_size("shard")
    factor = 1.0 / math.sqrt(total_tokens)
    cot_all = lax.all_gather(out_grad, "shard", axis=0, tiled=True)
    gate_cols, up_cols = (
        lax.all_to_all(gate_pre, "shard", split_axis=1, concat_axis=0, tiled=True),
        lax.all_to_all(up_pre, "shard", split_axis=1, concat_axis=0, tiled=True),
    )
    d_hidden = jnp.dot(cot_all, w_down, preferred_element_type=jnp.float32)
    hidden, d_stack = local_grads(
        gate_cols.astype(jnp.float32), up_cols.astype(jnp.float32), d_hidden
    )
    d_gate_up = lax.all_to_all(d_stack, "shard", split_axis=0, concat_axis=2, tiled=True)
    grad_rows = lax.psum_scatter(
        contract_rows(cot_all, hidden) * factor, "replica", scatter_dimension=0, tiled=True
    )
    dir_rows, first_down, second_down = adam_step(m_down, v_down, grad_rows)
    direction_down = lax.all_gather(dir_rows, "replica", axis=0, tiled=True)
    return (d_gate_up, direction_down, first_down, second_down)


def solution(mesh):
    return jax.shard_map(
        local,
        mesh=mesh,
        in_specs=(
            P(("replica", "shard"), None),
            P(("replica", "shard"), None),
            P(("replica", "shard"), None),
            P(None, "shard"),
            P("replica", "shard"),
            P("replica", "shard"),
        ),
        out_specs=(
            P(("replica", "shard"), None, None),
            P(None, "shard"),
            P("replica", "shard"),
            P("replica", "shard"),
        ),
        check_vma=False,
    )
```

profile of v0, /device:TPU:1, one launch (start us, length us, event | category | flops | bytes accessed | tf_op | source)
XLA Modules:
  0.0 451.4 jit_solution(6177514488994781332)
XLA Ops:
  7.2 0.0 copy-start.2
  7.2 0.0 all-gather.3.cloned.1.call-start
  7.2 0.7 all-gather.3.cloned.1.call-update
  7.9 0.4 copy-done.2
  8.3 0.0 copy-start.3
  8.3 1.3 copy.25
  9.6 6.4 %all-to-all-start = ((bf16[128,8,448]{0,2,1:T(8,128)(2,1)}), bf16[128,8,448]{0,2,1:T(8,128)(2,1)S(1)}, u32[]{:S(2)}, u32[]{:S(2)}) async-start(bf16[128,8,448]{0,2,1:T(8,128)(2,1)} %bitcast), calls=%async_computation | async-start | bytes 1835008 | tf_op jit(solution)/shard_map/all_to_all | solution.py:43
  16.0 0.0 reduce-scatter.2.cloned.1.call-start
  16.0 0.0 copy-done.3
  16.0 0.6 copy.27
  16.7 17.4 %all-to-all-done = bf16[128,8,448]{0,2,1:T(8,128)(2,1)S(1)} async-done(((bf16[128,8,448]{0,2,1:T(8,128)(2,1)}), bf16[128,8,448]{0,2,1:T(8,128)(2,1)S(1)}, u32[]{:S(2)}, u32[]{:S(2)}) %all-to-all-start) | async-done | bytes 917536 | tf_op jit(solution)/shard_map/all_to_all | solution.py:43
  34.1 27.6 %all_to_all.44 = bf16[128,8,448]{0,2,1:T(8,128)(2,1)S(1)} all-to-all(bf16[128,8,448]{0,2,1:T(8,128)(2,1)S(1)} %bitcast.69), channel_id=1, replica_groups=mesh['replica'=16,'shard'=8] {'shard'}, dimensions={1} | all-to-all | bytes 1835008 | tf_op jit(solution)/shard_map/all_to_all | solution.py:42
  61.7 0.0 copy-start.4
  61.7 136.8 %all-gather.3.cloned.1.call-done = bf16[1024,8192]{1,0:T(8,128)(2,1)} async-done(((bf16[128,8192]{1,0:T(8,128)(2,1)}), bf16[1024,8192]{1,0:T(8,128)(2,1)}) %all-gather.3.cloned.1.call-update) | async-done | bytes 16777232 | tf_op jit(solution)/shard_map/all_gather | solution.py:40
  198.5 17.0 %multiply_bitcast_fusion = f32[8192,448]{0,1:T(8,128)} fusion(bf16[1024,8192]{1,0:T(8,128)(2,1)} %all-gather.3.cloned.1.call-done, bf16[128,8,448]{0,2,1:T(8,128)(2,1)S(1)} %all-to-all-done, bf16[128,8,448]{0,2,1:T(8,128)(2,1)S(1)} %all_to_all.44), kind=kOutput, calls=%fused_computation | convolution fusion | flops 7523532800 | bytes 33292288 | tf_op jit(solution)/shard_map/dot_general | solution.py:25
  215.5 0.0 copy-done.4
  215.5 0.0 copy-start
  215.5 0.0 reduce-scatter.2.cloned.1.call-update
  215.5 0.0 all-gather.5.cloned.1.call-start
  215.6 131.1 %reduce-scatter.2.cloned.1.call-done = f32[512,448]{0,1:T(8,128)} async-done(((f32[8192,448]{0,1:T(8,128)}), f32[512,448]{0,1:T(8,128)}) %reduce-scatter.2.cloned.1.call-update) | async-done | bytes 917520 | tf_op jit(solution)/shard_map/reduce_scatter | solution.py:50
  346.7 0.0 copy-done
  346.7 0.0 copy-done.1
  346.7 3.0 divide_convert_fusion
  349.7 0.0 all-gather.5.cloned.1.call-update
  349.7 16.6 %fusion.11 = (bf16[1024,1,448]{0,2,1:T(8,128)(2,1)S(1)}, bf16[1024,1,448]{0,2,1:T(8,128)(2,1)S(1)}) fusion(bf16[1024,8192]{1,0:T(8,128)(2,1)} %all-gather.3.cloned.1.call-done, bf16[8192,448]{0,1:T(8,128)(2,1)} %param.9, bf16[128,8,448]{0,2,1:T(8,128)(2,1)S(1)} %all-to-all-done, bf16[128,8,448]{0,2,1:T(8,128)(2,1)} %copy-done.4), kind=kOutput, calls=%fused_computation.23 | convolution fusion | flops 7523074048 | bytes 27787264 | tf_op jit(solution)/shard_map/dot_general | solution.py:45
  366.2 1.4 pad_maximum_fusion
  367.6 4.8 %copy.29 = bf16[1024,2,448]{2,1,0:T(2,128)(2,1)S(1)} copy(bf16[1024,2,448]{0,2,1:T(8,128)(2,1)} %pad_maximum_fusion) | data formatting | bytes 3670016 | tf_op jit(solution)/shard_map/stack | solution.py:21
  372.4 29.7 %all_to_all.45 = bf16[1024,2,448]{2,1,0:T(2,128)(2,1)} all-to-all(bf16[1024,2,448]{2,1,0:T(2,128)(2,1)S(1)} %copy.29), channel_id=1, replica_groups=mesh['replica'=16,'shard'=8] {'shard'}, dimensions={0} | all-to-all | bytes 3670016 | tf_op jit(solution)/shard_map/all_to_all | solution.py:49
  402.1 4.9 %copy.34 = bf16[8,128,2,448]{1,3,0,2:T(8,128)(2,1)S(1)} copy(bf16[8,128,2,448]{3,2,1,0:T(2,128)(2,1)} %bitcast.67) | data formatting | bytes 3670016 | tf_op jit(solution)/shard_map/all_to_all | solution.py:49
  407.0 3.6 copy.32
  410.6 27.3 %all-gather.5.cloned.1.call-done = bf16[8192,448]{0,1:T(8,128)(2,1)} async-done(((bf16[512,448]{0,1:T(8,128)(2,1)}), bf16[8192,448]{0,1:T(8,128)(2,1)}) %all-gather.5.cloned.1.call-update) | async-done | bytes 7340048 | tf_op jit(solution)/shard_map/all_gather | solution.py:54
  437.9 7.0 %copy.52 = bf16[8192,448]{0,1:T(8,128)(2,1)} copy(bf16[8192,448]{0,1:T(8,128)(2,1)} %all-gather.5.cloned.1.call-done) | data formatting | bytes 14680064
  (1 shorter events, 0.0 us)
Async XLA Ops:
  7.2 1.2 copy-start.2
  7.2 191.3 %all-gather.3.cloned.1.call-start = ((), (), s32[]{:S(2)}) async-start(), calls=%async_computation.4 | async-start | bytes 18874368 | tf_op jit(solution)/shard_map/all_gather | solution.py:40
  8.3 7.7 %copy-start.3 = (bf16[128,3584]{1,0:T(8,128)(2,1)S(1)}, bf16[128,3584]{1,0:T(8,128)(2,1)}, u32[]{:S(2)}) copy-start(bf16[128,3584]{1,0:T(8,128)(2,1)} %param.6) | copy-start | bytes 2752516
  9.6 24.5 %all-to-all-start = ((bf16[128,8,448]{0,2,1:T(8,128)(2,1)}), bf16[128,8,448]{0,2,1:T(8,128)(2,1)S(1)}, u32[]{:S(2)}, u32[]{:S(2)}) async-start(bf16[128,8,448]{0,2,1:T(8,128)(2,1)} %bitcast), calls=%async_computation | async-start | bytes 1835008 | tf_op jit(solution)/shard_map/all_to_all | solution.py:43
  16.0 330.7 %reduce-scatter.2.cloned.1.call-start = ((), (), s32[]{:S(2)}) async-start(), calls=%async_computation.5 | async-start | bytes 15597568 | tf_op jit(solution)/shard_map/reduce_scatter | solution.py:50
  61.7 153.8 %copy-start.4 = (bf16[128,8,448]{0,2,1:T(8,128)(2,1)}, bf16[128,8,448]{0,2,1:T(8,128)(2,1)S(1)}, u32[]{:S(2)}) copy-start(bf16[128,8,448]{0,2,1:T(8,128)(2,1)S(1)} %all_to_all.44) | copy-start | bytes 2752516
  215.5 131.1 %copy-start = (f32[512,448]{0,1:T(8,128)S(1)}, f32[512,448]{0,1:T(8,128)}, u32[]{:S(2)}) copy-start(f32[512,448]{0,1:T(8,128)} %param.10) | copy-start | bytes 2752516
  215.5 131.1 %copy-start.1 = (f32[512,448]{0,1:T(8,128)S(1)}, f32[512,448]{0,1:T(8,128)}, u32[]{:S(2)}) copy-start(f32[512,448]{0,1:T(8,128)} %param.11) | copy-start | bytes 2752516
  215.5 222.4 %all-gather.5.cloned.1.call-start = ((), (), s32[]{:S(2)}) async-start(), calls=%async_computation.6 | async-start | bytes 7798784 | tf_op jit(solution)/shard_map/all_gather | solution.py:54
Sparse Core Ops, SparseCore 0:
  9.7 188.8 all-gather.2
  215.7 130.9 reduce-scatter.1
  349.8 88.0 all-gather.4
where the time goes:
time: 452 us; the launch traced here: 451 us
  waiting for transfers between devices  313 us (69%)
  blocking collectives  57.3 us (13%)
  matrix products  33.6 us (7%)
  local copies, waits for them, and re-layouts  22.6 us (5%)
  between operations  13.8 us (3%)
  starting transfers between devices  6.49 us (1%)
    all_gather x1, waiting for transfers between devices, local(): cot_all = lax.all_gather(out_grad, 'shard', axis=0, tiled=True)  137 us
    reduce_scatter x1, waiting for transfers between devices, local(): lax.psum_scatter(contract_rows(cot_all, hidden) * factor, 'replica', scat...  131 us
    all_to_all x1, blocking collectives, local(): lax.all_to_all(d_stack, 'shard', split_axis=0, concat_axis=2, tiled=True)  29.7 us
    all_to_all x1, blocking collectives, local(): lax.all_to_all(gate_pre, 'shard', split_axis=1, concat_axis=0, tiled=True)  27.6 us
    all_gather x1, waiting for transfers between devices, local(): direction_down = lax.all_gather(dir_rows, 'replica', axis=0, tiled=True)  27.3 us
    all_to_all x1, waiting for transfers between devices, local(): lax.all_to_all(up_pre, 'shard', split_axis=1, concat_axis=0, tiled=True)  17.4 us
    dot_general x1, matrix products, contract_rows(): lax.dot_general(left, right, (((0,), (0,)), ((), ())), preferred_element_...  17 us
    dot_general x1, matrix products, local(): d_hidden = jnp.dot(cot_all, w_down, preferred_element_type=jnp.float32)  16.6 us
  transfers between devices with their start and end apart: 4, of which 4 were waited for; matrix products, arithmetic and copies ran while one was open for 7% of the time, Pallas kernels for 0%

commit v1 on v0

v1 whole, which is shorter than its diff:
```python
import math

import jax
import jax.numpy as jnp
from jax import lax
from jax.experimental import pallas as pl
from jax.experimental.pallas import tpu as pltpu
from jax.sharding import PartitionSpec as P

beta_one = 0.9
beta_two = 0.95
epsilon = 1e-08
bias_one = 1.0 - beta_one**10
bias_two = 1.0 - beta_two**10

MESH = pl.DeviceIdType.MESH
BF = jnp.bfloat16
F32 = jnp.float32

TB = 128
HB = 448
ROWS = 512
TILE = 128
X_ORDER = (2, 1, 3, 0)
Y_ORDER = (2, 1, 3, 0)
STEPS = [(t, j) for t in range(2) for j in X_ORDER]


def kernel(
    gate, up, og, w, m, v,
    dgu, dirs, first, second,
    hid_own, hid, ogb, wbuf, rs_send, rs_recv, own, zs_send, zs_recv, gk, sw_send, sw_recv, dir_own,
    dk, cs_send, cs_recv, zd_send, zd_recv, yd_send, yd_recv,
    s1_s, s1_r, s2_s, s2_r, fw_s, fw_r, h1_s, h1_r, h2_s, h2_r, h3_s, h3_r, w_s, w_r, w_l,
    rs_s, rs_r, zs_s, zs_r, sw_s, sw_r, a_l, a_s, a_r, b_s, b_r, c_s, c_r,
    cs_s, cs_r, zd_s, zd_r, yd_s, yd_r,
):
    rep, sh = lax.axis_index("replica"), lax.axis_index("shard")
    zh, x, c = rep // 8, (rep // 2) % 4, rep % 2
    zl, y = sh // 4, sh % 4
    q = zl * 2 + c
    factor = 1.0 / math.sqrt(TB * 128)
    sends = []

    def dev(dzh=0, dx=0, dc=0, dzl=0, dy=0):
        return {
            "replica": ((zh + dzh) % 2) * 8 + ((x + dx) % 4) * 2 + (c + dc) % 2,
            "shard": ((zl + dzl) % 2) * 4 + (y + dy) % 4,
        }

    def push(src, dst, ssem, rsem, to, keep=True):
        cp = pltpu.make_async_remote_copy(
            src_ref=src, dst_ref=dst, send_sem=ssem, recv_sem=rsem, device_id=to, device_id_type=MESH
        )
        cp.start()
        if keep:
            sends.append((src, ssem))

    def landed(ref, sem):
        pltpu.make_async_copy(ref, ref, sem).wait()

    for i in range(28):
        cols = pl.ds(i * 128, 128)
        g = gate[:, cols].astype(F32)
        u = up[:, cols].astype(F32)
        hid_own[cols, :] = (g * jax.nn.sigmoid(g) * u).T.astype(BF)

    peers = [dev(dc=1), dev(dzl=1), dev(dzl=1, dc=1), dev(dzh=1), dev(dzh=1, dzl=1)]
    peers += [dev(dy=d) for d in (1, 2, 3)] + [dev(dx=d) for d in (1, 2, 3)]
    barrier = pltpu.get_barrier_semaphore()
    for peer in peers:
        pl.semaphore_signal(barrier, inc=1, device_id=peer, device_id_type=MESH)
    pl.semaphore_wait(barrier, len(peers))

    def tok(yy, qq):
        return pl.ds(pl.multiple_of((yy * 4 + qq) * TB, TB), TB)

    for n, dy in enumerate((2, 1, 3)):
        yd = (y + dy) % 4
        for b in range(2):
            rows = pl.ds(pl.multiple_of((b * 4 + yd) * HB, 16), HB)
            push(hid_own.at[rows, :], hid.at[b, :, tok(y, q)], h1_s.at[n, b], h1_r.at[n, b], dev(dy=dy))
    for b in range(2):
        rows = pl.ds(pl.multiple_of((b * 4 + y) * HB, 16), HB)
        pltpu.make_async_copy(hid_own.at[rows, :], hid.at[b, :, tok(y, q)], h1_r.at[3, b]).start()

    def d_row(zh2, dx, c2, zl2, t):
        r = zh2 * 8 + ((x + dx) % 4) * 2 + c2
        return pl.multiple_of(r * ROWS + zl2 * 256 + t * TILE, TILE)

    for k, (t, j) in enumerate(STEPS):
        for dzl, dc in ((1, 0), (1, 1), (0, 1), (0, 0)):
            for z in range(2):
                cols = pl.ds(d_row(z, j, (c + dc) % 2, (zl + dzl) % 2, t), TILE)
                dst = ogb.at[k, tok(y, q), pl.ds(z * TILE, TILE)]
                if dzl or dc:
                    push(og.at[:, cols], dst, s1_s.at[k], s1_r.at[k, q], dev(dc=dc, dzl=dzl), keep=False)
                else:
                    pltpu.make_async_copy(og.at[:, cols], dst, s1_r.at[k, q]).start()

    def slot(yy, lo=0, n=512):
        return pl.ds(pl.multiple_of(yy * 512 + lo, 128), n)

    def spread(k):
        for qq in range(4):
            landed(ogb.at[k, tok(y, qq), :], s1_r.at[k, qq])
        for n, dy in enumerate((1, 3)):
            push(ogb.at[k, slot(y), :], ogb.at[k, slot(y), :], s2_s.at[k, n], s2_r.at[k, n], dev(dy=dy))

    for k in range(2):
        spread(k)

    for n in range(4):
        ys = (y - (2, 1, 3, 0)[n]) % 4
        for b in range(2):
            landed(hid.at[b, :, tok(ys, q)], h1_r.at[n, b])
        blk = hid.at[:, :, tok(ys, q)]
        push(blk, blk, h2_s.at[n, 0], h2_r.at[n, 0], dev(dzl=1))
        push(blk, blk, h2_s.at[n, 1], h2_r.at[n, 1], dev(dc=1))

    for k in range(2, 8):
        spread(k)

    for n in range(4):
        ys = (y - (2, 1, 3, 0)[n]) % 4
        blk = hid.at[:, :, tok(ys, (1 - zl) * 2 + c)]
        landed(blk, h2_r.at[n, 0])
        push(blk, blk, h3_s.at[n], h3_r.at[n], dev(dc=1))
        landed(hid.at[:, :, tok(ys, zl * 2 + 1 - c)], h2_r.at[n, 1])

    for k, (t, j) in enumerate(STEPS):
        for z in range(2):
            half = pl.ds(z * TILE, TILE)
            mine = pl.ds(d_row(z, j, c, zl, t), TILE)
            theirs = pl.ds(d_row(z, j, c, 1 - zl, t), TILE)
            pltpu.make_async_copy(w.at[mine, :], wbuf.at[k, zl, half, :], w_l).start()
            push(w.at[theirs, :], wbuf.at[k, zl, half, :], w_s.at[t], w_r.at[t], dev(dzl=1, dzh=t), keep=False)

    for n in range(4):
        ys = (y - (2, 1, 3, 0)[n]) % 4
        landed(hid.at[:, :, tok(ys, (1 - zl) * 2 + 1 - c)], h3_r.at[n])

    def forward(k):
        down, upw = (y + 3) % 4, (y + 1) % 4
        landed(ogb.at[k, slot(down), :], s2_r.at[k, 0])
        part = ogb.at[k, slot(down, 0, 256), :]
        push(part, part, fw_s.at[k, 0], fw_r.at[k, 0], dev(dy=1))
        landed(ogb.at[k, slot(upw), :], s2_r.at[k, 1])
        part = ogb.at[k, slot(upw, 256, 256), :]
        push(part, part, fw_s.at[k, 1], fw_r.at[k, 1], dev(dy=3))

    def grad(k):
        t, j = STEPS[k]
        far = (y + 2) % 4
        landed(ogb.at[k, slot(far, 0, 256), :], fw_r.at[k, 0])
        landed(ogb.at[k, slot(far, 256, 256), :], fw_r.at[k, 1])

        @pl.loop(0, 2)
        def _(b):
            prod = jnp.dot(hid[b], ogb[k], preferred_element_type=F32)
            for z in range(2):
                part = prod[:, z * TILE : (z + 1) * TILE]
                if j:
                    rs_send[t, j - 1, z, b] = part.astype(BF)
                else:
                    own[t, z, b] = part

        if j:
            push(rs_send.at[t, j - 1], rs_recv.at[t, j - 1], rs_s.at[t, j - 1], rs_r.at[t, j - 1], dev(dx=j))

    def x_sum(t):
        for j in (1, 2, 3):
            landed(rs_recv.at[t, j - 1], rs_r.at[t, j - 1])

        @pl.loop(0, 2)
        def _(b):
            for z, mine in ((zh, True), (1 - zh, False)):
                total = own[t, z, b]
                for j in range(3):
                    total += rs_recv[t, j, z, b].astype(F32)
                if mine:
                    own[t, z, b] = total
                else:
                    zs_send[t, b] = total.astype(BF)

        push(zs_send.at[t], zs_recv.at[t], zs_s.at[t], zs_r.at[t], dev(dzh=1))

    def z_sum(t):
        landed(zs_recv.at[t], zs_r.at[t])
        gk[t] = own[t, zh, zl] + zs_recv[t, zl].astype(F32)
        sw_send[t] = (own[t, zh, 1 - zl] + zs_recv[t, 1 - zl].astype(F32)).astype(BF)
        push(sw_send.at[t], sw_recv.at[t], sw_s.at[t], sw_r.at[t], dev(dzl=1))

    def adam(t):
        landed(sw_recv.at[t], sw_r.at[t])
        for half, g_units in ((zl, gk[t]), (1 - zl, sw_recv[t].astype(F32))):
            g = g_units.T * factor
            rows = pl.ds(pl.multiple_of(half * 256 + t * TILE, TILE), TILE)
            first_new = beta_one * m[rows, :] + (1.0 - beta_one) * g
            second_new = beta_two * v[rows, :] + (1.0 - beta_two) * g * g
            first[rows, :] = first_new
            second[rows, :] = second_new
            direction = first_new / bias_one / (jnp.sqrt(second_new / bias_two) + epsilon)
            dir_own[t, half] = direction.astype(BF)
        pltpu.make_async_copy(dir_own.at[t], dirs.at[c, t, x, zh], a_l.at[t]).start()
        push(dir_own.at[t], dirs.at[c, t, x, zh], a_s.at[t], a_r.at[t], dev(dzh=1))

    def dir_x(t):
        landed(dirs.at[c, t, x, zh], a_l.at[t])
        landed(dirs.at[c, t, x, 1 - zh], a_r.at[t])
        blk = dirs.at[c, t, x]
        for j in (2, 1, 3):
            push(blk, blk, b_s.at[t, j], b_r.at[t, j], dev(dx=j))
        push(blk, blk, c_s.at[t, 0], c_r.at[t, 0], dev(dc=1))

    def dir_core(t):
        for j in (1, 3, 2):
            blk = dirs.at[c, t, (x - j) % 4]
            landed(blk, b_r.at[t, j])
            push(blk, blk, c_s.at[t, j], c_r.at[t, j], dev(dc=1))

    def dir_end(t):
        for j in range(4):
            landed(dirs.at[1 - c, t, (x - j) % 4], c_r.at[t, j])

    def dh_dot(i):
        ys = (y + Y_ORDER[i]) % 4

        @pl.loop(0, 2)
        def _(b):
            total = None
            for k in range(8):
                part = jnp.dot(ogb[k, slot(ys), :], wbuf[k, b], preferred_element_type=F32)
                total = part if total is None else total + part
            ogs = total.reshape(2, 2, TB, HB)
            for zz in range(2):
                both = ogs[zz]
                dk[i, zz, b] = jnp.where(c == 0, both[0], both[1])
                cs_send[i, zz, b] = jnp.where(c == 0, both[1], both[0]).astype(BF)

        push(cs_send.at[i], cs_recv.at[i], cs_s.at[i], cs_r.at[i], dev(dc=1))

    def dh_core(i):
        landed(cs_recv.at[i], cs_r.at[i])

        @pl.loop(0, 2)
        def _(b):
            dk[i, zl, b] = dk[i, zl, b] + cs_recv[i, zl, b].astype(F32)
            zd_send[i, b] = (dk[i, 1 - zl, b] + cs_recv[i, 1 - zl, b].astype(F32)).astype(BF)

        push(zd_send.at[i], zd_recv.at[i], zd_s.at[i], zd_r.at[i], dev(dzl=1))

    def dh_z(i):
        landed(zd_recv.at[i], zd_r.at[i])
        dy = Y_ORDER[i]
        for b in range(2):
            total = (dk[i, zl, b] + zd_recv[i, b].astype(F32)).astype(BF)
            if dy:
                yd_send[i, b] = total
            else:
                yd_recv[y, b] = total
        if dy:
            push(yd_send.at[i], yd_recv.at[y], yd_s.at[i], yd_r.at[i], dev(dy=dy))

    forward(0)
    for k in range(8):
        if k < 7:
            forward(k + 1)
        grad(k)
        if k == 5:
            x_sum(0)
        if k == 6:
            z_sum(0)
        if k == 7:
            adam(0)
    x_sum(1)
    landed(wbuf.at[:, zl], w_l)
    for t in range(2):
        landed(wbuf.at[pl.ds(t * 4, 4), 1 - zl], w_r.at[t])
    dh_dot(0)
    z_sum(1)
    dir_x(0)
    dh_dot(1)
    dh_core(0)
    adam(1)
    dh_dot(2)
    dh_core(1)
    dh_z(0)
    dir_x(1)
    dh_dot(3)
    dh_core(2)
    dh_z(1)
    dir_core(0)
    dh_core(3)
    dh_z(2)
    dh_z(3)
    for i in range(3):
        ys = (y - Y_ORDER[i]) % 4
        landed(yd_recv.at[ys], yd_r.at[i])
    for b in range(2):
        for ys in range(4):
            cols = pl.ds((b * 4 + ys) * HB, HB)
            d = yd_recv[ys, b].astype(F32)
            g = gate[:, cols].astype(F32)
            u = up[:, cols].astype(F32)
            sig = jax.nn.sigmoid(g)
            dgu[0, :, cols] = (d * u * sig * (1.0 + g * (1.0 - sig))).astype(BF)
            dgu[1, :, cols] = (d * (g * sig)).astype(BF)
    dir_core(1)
    dir_end(0)
    dir_end(1)

    for src, sem in sends:
        landed(src, sem)
    for k in range(8):
        landed(ogb.at[k, pl.ds(0, 384), :], s1_s.at[k])
    for t in range(2):
        landed(wbuf.at[pl.ds(t * 4, 4), 0], w_s.at[t])


def local(gate_pre, up_pre, out_grad, w_down, m_down, v_down):
    vmem = pl.BlockSpec(memory_space=pltpu.VMEM)
    hbm = pl.BlockSpec(memory_space=pl.ANY)
    dma = pltpu.SemaphoreType.DMA
    scratch = [
        pltpu.VMEM((8 * HB, TB), BF),
        pltpu.VMEM((2, HB, 16 * TB), BF),
        pltpu.VMEM((8, 2048, 256), BF),
        pltpu.VMEM((8, 2, 256, HB), BF),
        pltpu.VMEM((2, 3, 2, 2, HB, TILE), BF),
        pltpu.VMEM((2, 3, 2, 2, HB, TILE), BF),
        pltpu.VMEM((2, 2, 2, HB, TILE), F32),
        pltpu.VMEM((2, 2, HB, TILE), BF),
        pltpu.VMEM((2, 2, HB, TILE), BF),
        pltpu.VMEM((2, HB, TILE), F32),
        pltpu.VMEM((2, HB, TILE), BF),
        pltpu.VMEM((2, HB, TILE), BF),
        pltpu.VMEM((2, 2, TILE, HB), BF),
        pltpu.VMEM((4, 2, 2, TB, HB), F32),
        pltpu.VMEM((4, 2, 2, TB, HB), BF),
        pltpu.VMEM((4, 2, 2, TB, HB), BF),
        pltpu.VMEM((4, 2, TB, HB), BF),
        pltpu.VMEM((4, 2, TB, HB), BF),
        pltpu.VMEM((3, 2, TB, HB), BF),
        pltpu.VMEM((4, 2, TB, HB), BF),
        dma((8,)), dma((8, 4)),
        dma((8, 2)), dma((8, 2)),
        dma((8, 2)), dma((8, 2)),
        dma((3, 2)), dma((4, 2)),
        dma((4, 2)), dma((4, 2)),
        dma((4,)), dma((4,)),
        dma((2,)), dma((2,)), dma,
        dma((2, 3)), dma((2, 3)),
        dma((2,)), dma((2,)),
        dma((2,)), dma((2,)),
        dma((2,)), dma((2,)), dma((2,)),
        dma((2, 4)), dma((2, 4)),
        dma((2, 4)), dma((2, 4)),
        dma((4,)), dma((4,)),
        dma((4,)), dma((4,)),
        dma((3,)), dma((3,)),
    ]
    dgu, dirs, first, second = pl.pallas_call(
        kernel,
        name="step",
        out_shape=(
            jax.ShapeDtypeStruct((2, TB, 8 * HB), BF),
            jax.ShapeDtypeStruct((2, 2, 4, 2, 2, TILE, HB), BF),
            jax.ShapeDtypeStruct((ROWS, HB), F32),
            jax.ShapeDtypeStruct((ROWS, HB), F32),
        ),
        in_specs=[vmem, vmem, vmem, hbm, vmem, vmem],
        out_specs=(vmem, hbm, vmem, vmem),
        scratch_shapes=scratch,
        compiler_params=pltpu.CompilerParams(
            collective_id=0, has_side_effects=True, vmem_limit_bytes=60 << 20
        ),
        cost_estimate=pl.CostEstimate(flops=15 * 10**9, bytes_accessed=40 * 10**6, transcendentals=0),
    )(gate_pre, up_pre, out_grad, w_down, m_down, v_down)
    direction = dirs.transpose(3, 2, 0, 4, 1, 5, 6).reshape(16 * ROWS, HB)
    return (dgu.transpose(1, 0, 2), direction, first, second)


def solution(mesh):
    return jax.shard_map(
        local,
        mesh=mesh,
        in_specs=(
            P(("replica", "shard"), None),
            P(("replica", "shard"), None),
            P(("replica", "shard"), None),
            P(None, "shard"),
            P("replica", "shard"),
            P("replica", "shard"),
        ),
        out_specs=(
            P(("replica", "shard"), None, None),
            P(None, "shard"),
            P("replica", "shard"),
            P("replica", "shard"),
        ),
        check_vma=False,
    )
```

time: 452 us -> 236 us (0.52)
  waiting for transfers between devices: 313 us -> 0 us
  Pallas kernels: 0 us -> 176 us
  blocking collectives: 57.3 us -> 0 us
  local copies, waits for them, and re-layouts: 22.6 us -> 57.3 us
  matrix products: 33.6 us -> 0 us
  between operations: 13.8 us -> 0.64 us
  starting transfers between devices: 6.49 us -> 0 us
    pallas_call x0 -> x1, Pallas kernels: none -> 176 us  [local(): pl.pallas_call(kernel, name='step', out_shape=(jax.ShapeDtypeStruct((2, T...]
    all_gather x2 -> x0, waiting for transfers between devices: 164 us -> none  [the longest x1 137 us: local(): cot_all = lax.all_gather(out_grad, 'shard', axis=0, tiled=True)]
    reduce_scatter x1 -> x0, waiting for transfers between devices: 131 us -> none  [local(): lax.psum_scatter(contract_rows(cot_all, hidden) * factor, 'replica', scat...]
    all_to_all x2 -> x0, blocking collectives: 57.3 us -> none  [the longest x1 29.7 us: local(): lax.all_to_all(d_stack, 'shard', split_axis=0, concat_axis=2, tiled=True)]
    dot_general x2 -> x0, matrix products: 33.6 us -> none  [the longest x1 17 us: contract_rows(): lax.dot_general(left, right, (((0,), (0,)), ((), ())), preferred_element_...]
    transpose x0 -> x1, local copies, waits for them, and re-layouts: none -> 21.3 us  [local(): direction = dirs.transpose(3, 2, 0, 4, 1, 5, 6).reshape(16 * ROWS, HB)]
    all_to_all x1 -> x0, waiting for transfers between devices: 17.4 us -> none  [local(): lax.all_to_all(up_pre, 'shard', split_axis=1, concat_axis=0, tiled=True)]
    reshape x0 -> x1, local copies, waits for them, and re-layouts: none -> 12.9 us  [local(): direction = dirs.transpose(3, 2, 0, 4, 1, 5, 6).reshape(16 * ROWS, HB)]
  transfers between devices with their start and end apart: 4 -> 0, of which waited for: 4 -> 0; matrix products, arithmetic and copies ran while one was open for 7% -> 0% of each run, Pallas kernels for 0% -> 0%
where the time goes in v1:
time: 236 us; the launch traced here: 234 us
  Pallas kernels  176 us (75%)
  local copies, waits for them, and re-layouts  57.3 us (24%)
    pallas_call x1, Pallas kernels, local(): pl.pallas_call(kernel, name='step', out_shape=(jax.ShapeDtypeStruct((2, T...  176 us
    unnamed x10, local copies, waits for them, and re-layouts  23.1 us
    transpose x1, local copies, waits for them, and re-layouts, local(): direction = dirs.transpose(3, 2, 0, 4, 1, 5, 6).reshape(16 * ROWS, HB)  21.3 us
    reshape x1, local copies, waits for them, and re-layouts, local(): direction = dirs.transpose(3, 2, 0, 4, 1, 5, 6).reshape(16 * ROWS, HB)  12.9 us

profile of v1, /device:TPU:1, one launch (start us, length us, event | category | flops | bytes accessed | tf_op | source)
XLA Modules:
  0.0 234.3 jit_solution(1301349188544470958)
XLA Ops:
  0.6 2.5 %copy.17.m = f32[512,448]{1,0:T(8,128)} copy(f32[512,448]{0,1:T(8,128)} %param.10) | data formatting | bytes 1835008 | tf_op args[4]
  3.1 2.5 %copy.18.v = f32[512,448]{1,0:T(8,128)} copy(f32[512,448]{0,1:T(8,128)} %param.11) | data formatting | bytes 1835008 | tf_op args[5]
  5.6 11.0 %copy.16.w = bf16[8192,448]{1,0:T(8,128)(2,1)} copy(bf16[8192,448]{0,1:T(8,128)(2,1)} %param.9) | data formatting | bytes 14680064 | tf_op args[3]
  16.6 176.4 %step.1 = (bf16[2,128,3584]{2,1,0:T(8,128)(2,1)}, bf16[2,2,4,2,2,128,448]{6,5,4,3,2,1,0:T(8,128)(2,1)}, f32[512,448]{1,0:T(8,128)}, f32[512,448]{1,0:T(8,128)}) custom-call(bf16[128,3584]{1,0:T(8,128)(2,1)} %gate.1, bf16[128,3584]{1,0:T(8,128)(2,1)} %up.1, bf16[128,8192]{1,0:T(8,128)(2,1)} %og.1, bf16[8192,448]{1,0:T(8,128)(2,1)} %copy.16.w, ...), custom_call_target="tpu_custom_call" | custom-call | flops 15000000512 | bytes 40000000 | tf_op jit(solution)/shard_map/step/pallas_call | solution.py:363
  193.0 4.6 %copy.20 = bf16[128,2,3584]{2,1,0:T(2,128)(2,1)} copy(bf16[128,2,3584]{2,0,1:T(8,128)(2,1)} %bitcast.5) | data formatting | bytes 3670016
  197.6 21.3 %copy.19 = bf16[2,4,2,2,2,128,448]{5,4,3,2,1,0,6:T(2,128)(2,1)} copy(bf16[2,4,2,2,2,128,448]{6,5,3,0,1,4,2:T(8,128)(2,1)} %bitcast.4) | data formatting | bytes 14680064 | tf_op jit(solution)/shard_map/transpose | solution.py:380
  218.9 0.0 copy-start.1
  218.9 0.0 copy-start
  218.9 12.9 %reshape.11 = bf16[8192,448]{0,1:T(8,128)(2,1)} reshape(bf16[2,4,2,2,2,128,448]{5,4,3,2,1,0,6:T(2,128)(2,1)} %copy.19) | data formatting | bytes 14680064 | tf_op jit(solution)/shard_map/reshape | solution.py:380
  231.8 0.0 copy-done.1
  231.9 1.2 copy.21
  233.1 0.0 copy-done
  233.1 1.2 copy.22
Async XLA Ops:
  218.9 12.9 %copy-start.1 = (f32[512,448]{1,0:T(8,128)S(1)}, f32[512,448]{1,0:T(8,128)}, u32[]{:S(2)}) copy-start(f32[512,448]{1,0:T(8,128)} %get-tuple-element.18) | copy-start | bytes 2752516
  218.9 14.2 %copy-start = (f32[512,448]{1,0:T(8,128)S(1)}, f32[512,448]{1,0:T(8,128)}, u32[]{:S(2)}) copy-start(f32[512,448]{1,0:T(8,128)} %get-tuple-element.19) | copy-start | bytes 2752516

commit v2 on v1

v2 whole, which is shorter than its diff:
```python
import math

import jax
import jax.numpy as jnp
from jax import lax
from jax.experimental import pallas as pl
from jax.experimental.pallas import tpu as pltpu
from jax.sharding import PartitionSpec as P

beta_one = 0.9
beta_two = 0.95
epsilon = 1e-08
bias_one = 1.0 - beta_one**10
bias_two = 1.0 - beta_two**10

MESH = pl.DeviceIdType.MESH
BF = jnp.bfloat16
F32 = jnp.float32

TB = 128
HB = 448
ROWS = 512
TILE = 128
X_ORDER = (2, 1, 3, 0)
Y_ORDER = (2, 1, 3, 0)
STEPS = [(t, j) for t in range(2) for j in X_ORDER]


def kernel(
    gate, up, og, w, m, v,
    dgu, dirs, first, second,
    hid_own, d_own, hid, ogb, wbuf, rs_send, rs_recv, own, zs_send, zs_recv, gk, dir_own,
    dk, cs_send, cs_recv, zd_send, zd_recv, yd_send, yd_recv,
    s1_s, s1_r, s2_s, s2_r, fw_s, fw_r, h1_s, h1_r, h2_s, h2_r, h3_s, h3_r, w_s, w_r, w_l,
    rs_s, rs_r, zs_s, zs_r, a_l, a_s, a_r, b_s, b_r, c_s, c_r,
    cs_s, cs_r, zd_s, zd_r, yd_s, yd_r,
):
    rep, sh = lax.axis_index("replica"), lax.axis_index("shard")
    zh, x, c = rep // 8, (rep // 2) % 4, rep % 2
    zl, y = sh // 4, sh % 4
    q = zl * 2 + c
    factor = 1.0 / math.sqrt(TB * 128)
    sends = []

    def dev(dzh=0, dx=0, dc=0, dzl=0, dy=0):
        return {
            "replica": ((zh + dzh) % 2) * 8 + ((x + dx) % 4) * 2 + (c + dc) % 2,
            "shard": ((zl + dzl) % 2) * 4 + (y + dy) % 4,
        }

    def push(src, dst, ssem, rsem, to, keep=True):
        cp = pltpu.make_async_remote_copy(
            src_ref=src, dst_ref=dst, send_sem=ssem, recv_sem=rsem, device_id=to, device_id_type=MESH
        )
        cp.start()
        if keep:
            sends.append((src, ssem))

    def landed(ref, sem):
        pltpu.make_async_copy(ref, ref, sem).wait()

    for i in range(28):
        cols = pl.ds(i * 128, 128)
        g = gate[:, cols].astype(F32)
        u = up[:, cols].astype(F32)
        hid_own[cols, :] = (g * jax.nn.sigmoid(g) * u).T.astype(BF)

    peers = [dev(dc=1), dev(dzl=1), dev(dzl=1, dc=1), dev(dzh=1), dev(dzh=1, dzl=1)]
    peers += [dev(dy=d) for d in (1, 2, 3)] + [dev(dx=d) for d in (1, 2, 3)]
    barrier = pltpu.get_barrier_semaphore()
    for peer in peers:
        pl.semaphore_signal(barrier, inc=1, device_id=peer, device_id_type=MESH)
    pl.semaphore_wait(barrier, len(peers))

    def tok(yy, qq):
        return pl.ds(pl.multiple_of((yy * 4 + qq) * TB, TB), TB)

    def d_row(zh2, dx, c2, zl2, t):
        r = zh2 * 8 + ((x + dx) % 4) * 2 + c2
        return pl.multiple_of(r * ROWS + t * 256 + zl2 * TILE, TILE)

    def slot(yy, lo=0, n=512):
        return pl.ds(pl.multiple_of(yy * 512 + lo, 128), n)

    H_ORDER = (0, 1, 3, 2)

    def hid_y(n):
        dy = H_ORDER[n]
        for b in range(2):
            rows = pl.ds(pl.multiple_of((b * 4 + (y + dy) % 4) * HB, 16), HB)
            src, dst = hid_own.at[rows, :], hid.at[b, :, tok(y, q)]
            if dy:
                push(src, dst, h1_s.at[n, b], h1_r.at[n, b], dev(dy=dy))
            else:
                pltpu.make_async_copy(src, dst, h1_r.at[n, b]).start()

    def hid_z(n):
        ys = (y - H_ORDER[n]) % 4
        for b in range(2):
            landed(hid.at[b, :, tok(ys, q)], h1_r.at[n, b])
        blk = hid.at[:, :, tok(ys, q)]
        push(blk, blk, h2_s.at[n, 0], h2_r.at[n, 0], dev(dzl=1))
        push(blk, blk, h2_s.at[n, 1], h2_r.at[n, 1], dev(dc=1))

    def hid_core(n):
        ys = (y - H_ORDER[n]) % 4
        blk = hid.at[:, :, tok(ys, (1 - zl) * 2 + c)]
        landed(blk, h2_r.at[n, 0])
        push(blk, blk, h3_s.at[n], h3_r.at[n], dev(dc=1))

    def hid_end(n):
        ys = (y - H_ORDER[n]) % 4
        landed(hid.at[:, :, tok(ys, zl * 2 + 1 - c)], h2_r.at[n, 1])
        landed(hid.at[:, :, tok(ys, (1 - zl) * 2 + 1 - c)], h3_r.at[n])

    def quarter(k):
        t, j = STEPS[k]
        for dzl, dc in ((1, 0), (1, 1), (0, 1), (0, 0)):
            for z in range(2):
                cols = pl.ds(d_row(z, j, (c + dc) % 2, (zl + dzl) % 2, t), TILE)
                dst = ogb.at[k, tok(y, q), pl.ds(z * TILE, TILE)]
                if dzl or dc:
                    push(og.at[:, cols], dst, s1_s.at[k], s1_r.at[k, q], dev(dc=dc, dzl=dzl), keep=False)
                else:
                    pltpu.make_async_copy(og.at[:, cols], dst, s1_r.at[k, q]).start()

    def spread(k):
        for qq in range(4):
            landed(ogb.at[k, tok(y, qq), :], s1_r.at[k, qq])
        for n, dy in enumerate((1, 3)):
            push(ogb.at[k, slot(y), :], ogb.at[k, slot(y), :], s2_s.at[k, n], s2_r.at[k, n], dev(dy=dy))

    def weights():
        for k, (t, j) in enumerate(STEPS):
            for z in range(2):
                half = pl.ds(z * TILE, TILE)
                mine = pl.ds(d_row(z, j, c, zl, t), TILE)
                theirs = pl.ds(d_row(z, j, c, 1 - zl, t), TILE)
                pltpu.make_async_copy(w.at[:, mine], wbuf.at[k, zl, :, half], w_l).start()
                push(w.at[:, theirs], wbuf.at[k, zl, :, half], w_s.at[t], w_r.at[t], dev(dzl=1, dzh=t), keep=False)

    def forward(k):
        down, upw = (y + 3) % 4, (y + 1) % 4
        landed(ogb.at[k, slot(down), :], s2_r.at[k, 0])
        part = ogb.at[k, slot(down, 0, 256), :]
        push(part, part, fw_s.at[k, 0], fw_r.at[k, 0], dev(dy=1))
        landed(ogb.at[k, slot(upw), :], s2_r.at[k, 1])
        part = ogb.at[k, slot(upw, 256, 256), :]
        push(part, part, fw_s.at[k, 1], fw_r.at[k, 1], dev(dy=3))

    def grad(k):
        t, j = STEPS[k]
        far = (y + 2) % 4
        landed(ogb.at[k, slot(far, 0, 256), :], fw_r.at[k, 0])
        landed(ogb.at[k, slot(far, 256, 256), :], fw_r.at[k, 1])

        @pl.loop(0, 2)
        def _(b):
            prod = jnp.dot(hid[b], ogb[k], preferred_element_type=F32)
            for z in range(2):
                part = prod[:, z * TILE : (z + 1) * TILE]
                if j:
                    rs_send[t, j - 1, z, b] = part.astype(BF)
                else:
                    own[t, z, b] = part

        if j:
            push(rs_send.at[t, j - 1], rs_recv.at[t, j - 1], rs_s.at[t, j - 1], rs_r.at[t, j - 1], dev(dx=j))

    def x_sum(t):
        for j in (1, 2, 3):
            landed(rs_recv.at[t, j - 1], rs_r.at[t, j - 1])

        def total(z, b):
            out = own[t, z, b]
            for j in range(3):
                out += rs_recv[t, j, z, b].astype(F32)
            return out

        for n, (z, b) in enumerate(((1 - zh, zl), (zh, 1 - zl), (1 - zh, 1 - zl))):
            zs_send[t, n] = total(z, b).astype(BF)
            to = (dev(dzh=1), dev(dzl=1), dev(dzh=1, dzl=1))[n]
            push(zs_send.at[t, n], zs_recv.at[t, n], zs_s.at[t, n], zs_r.at[t, n], to)
        gk[t] = total(zh, zl)

    def block(zh2, x2, c2, t):
        r = zh2 * 8 + x2 * 2 + c2
        return dirs.at[:, pl.ds(pl.multiple_of(r * ROWS + t * 256, 256), 256)]

    def adam(t):
        for n in range(3):
            landed(zs_recv.at[t, n], zs_r.at[t, n])
        mine = gk[t] + zs_recv[t, 0].astype(F32)
        others = zs_recv[t, 1].astype(F32) + zs_recv[t, 2].astype(F32)
        for half, g_sum in ((zl, mine), (1 - zl, others)):
            g = g_sum * factor
            cols = pl.ds(pl.multiple_of(t * 256 + half * TILE, TILE), TILE)
            first_new = beta_one * m[:, cols] + (1.0 - beta_one) * g
            second_new = beta_two * v[:, cols] + (1.0 - beta_two) * g * g
            first[:, cols] = first_new
            second[:, cols] = second_new
            direction = first_new / bias_one / (jnp.sqrt(second_new / bias_two) + epsilon)
            dir_own[t, :, pl.ds(pl.multiple_of(half * TILE, TILE), TILE)] = direction.astype(BF)
        place, src = block(zh, x, c, t), dir_own.at[t]
        push(src, place, a_s.at[t], a_r.at[t], dev(dzh=1))
        for j in (2, 1, 3):
            push(src, place, b_s.at[t, j, 0], b_r.at[t, j, 0], dev(dx=j))
        push(src, place, c_s.at[t, 0, 0], c_r.at[t, 0, 0], dev(dc=1))
        pltpu.make_async_copy(src, place, a_l.at[t]).start()

    def dir_x(t):
        blk = block(1 - zh, x, c, t)
        landed(blk, a_r.at[t])
        for j in (2, 1, 3):
            push(blk, blk, b_s.at[t, j, 1], b_r.at[t, j, 1], dev(dx=j))
        push(blk, blk, c_s.at[t, 0, 1], c_r.at[t, 0, 1], dev(dc=1))

    def dir_core(t, n):
        for j in (1, 3, 2):
            blk = block(zh if n == 0 else 1 - zh, (x - j) % 4, c, t)
            landed(blk, b_r.at[t, j, n])
            push(blk, blk, c_s.at[t, j, n], c_r.at[t, j, n], dev(dc=1))

    def dir_end(t):
        landed(block(zh, x, c, t), a_l.at[t])
        for j in range(4):
            for n in range(2):
                landed(block(zh if n == 0 else 1 - zh, (x - j) % 4, 1 - c, t), c_r.at[t, j, n])

    def dh_dots(i, b, ks):
        total = None
        for k in ks:
            part = lax.dot_general(
                wbuf[k, b], ogb[k, slot((y + Y_ORDER[i]) % 4), :],
                (((1,), (1,)), ((), ())), preferred_element_type=F32,
            )
            total = part if total is None else total + part
        return total

    def dh_early(i):
        @pl.loop(0, 2)
        def _(b):
            dk[i, b] = dh_dots(i, b, range(4))

    def lanes(zz):
        return pl.ds(pl.multiple_of(zz * TB, TB), TB)

    def dh_late(i):
        @pl.loop(0, 2)
        def _(b):
            total = dh_dots(i, b, range(4, 8)) + dk[i, b]
            for zz in range(2):
                lo = total[:, zz * 256 : zz * 256 + 128]
                hi = total[:, zz * 256 + 128 : zz * 256 + 256]
                dk[i, b, :, lanes(zz)] = jnp.where(c == 0, lo, hi)
                cs_send[i, zz, b] = jnp.where(c == 0, hi, lo).astype(BF)

        push(cs_send.at[i], cs_recv.at[i], cs_s.at[i], cs_r.at[i], dev(dc=1))

    def dh_core(i):
        landed(cs_recv.at[i], cs_r.at[i])

        @pl.loop(0, 2)
        def _(b):
            dk[i, b, :, lanes(zl)] = dk[i, b, :, lanes(zl)] + cs_recv[i, zl, b].astype(F32)
            zd_send[i, b] = (dk[i, b, :, lanes(1 - zl)] + cs_recv[i, 1 - zl, b].astype(F32)).astype(BF)

        push(zd_send.at[i], zd_recv.at[i], zd_s.at[i], zd_r.at[i], dev(dzl=1))

    def dh_z(i):
        landed(zd_recv.at[i], zd_r.at[i])
        dy = Y_ORDER[i]
        for b in range(2):
            total = (dk[i, b, :, lanes(zl)] + zd_recv[i, b].astype(F32)).astype(BF)
            if dy:
                yd_send[i, b] = total
            else:
                yd_recv[y, b] = total
        if dy:
            push(yd_send.at[i], yd_recv.at[y], yd_s.at[i], yd_r.at[i], dev(dy=dy))

    def cotangents():
        for i in range(3):
            ys = (y - Y_ORDER[i]) % 4
            landed(yd_recv.at[ys], yd_r.at[i])
        for b in range(2):
            for ys in range(4):
                d_own[pl.ds((b * 4 + ys) * HB, HB), :] = yd_recv[ys, b]
        for i in range(28):
            cols = pl.ds(i * 128, 128)
            d = d_own[cols, :].astype(F32).T
            g = gate[:, cols].astype(F32)
            u = up[:, cols].astype(F32)
            sig = jax.nn.sigmoid(g)
            dgu[0, :, cols] = (d * u * sig * (1.0 + g * (1.0 - sig))).astype(BF)
            dgu[1, :, cols] = (d * (g * sig)).astype(BF)

    for n in range(1, 4):
        hid_y(n)
    hid_y(0)
    quarter(0)
    hid_z(0)
    quarter(1)
    quarter(2)
    spread(0)
    spread(1)
    hid_z(1)
    quarter(3)
    hid_z(2)
    quarter(4)
    hid_core(0)
    hid_z(3)
    for k in (5, 6, 7):
        quarter(k)
    forward(0)
    spread(2)
    hid_core(1)
    forward(1)
    spread(3)
    hid_core(2)
    forward(2)
    spread(4)
    hid_core(3)
    weights()
    for n in range(4):
        hid_end(n)
    grad(0)
    grad(1)
    forward(3)
    spread(5)
    grad(2)
    forward(4)
    spread(6)
    grad(3)
    landed(wbuf.at[:, zl], w_l)
    landed(wbuf.at[pl.ds(0, 4), 1 - zl], w_r.at[0])
    dh_early(0)
    forward(5)
    spread(7)
    grad(4)
    x_sum(0)
    dh_early(1)
    forward(6)
    grad(5)
    adam(0)
    dh_early(2)
    forward(7)
    grad(6)
    dir_x(0)
    dh_early(3)
    grad(7)
    landed(wbuf.at[pl.ds(4, 4), 1 - zl], w_r.at[1])
    dh_late(0)
    x_sum(1)
    dh_late(1)
    dh_core(0)
    dh_late(2)
    dh_core(1)
    adam(1)
    dh_late(3)
    dh_z(0)
    dh_core(2)
    dir_x(1)
    dir_core(0, 0)
    dir_core(0, 1)
    dh_z(1)
    dh_core(3)
    dh_z(2)
    dh_z(3)
    dir_core(1, 0)
    cotangents()
    dir_core(1, 1)
    dir_end(0)
    dir_end(1)

    for src, sem in sends:
        landed(src, sem)
    for k in range(8):
        landed(ogb.at[k, pl.ds(0, 384), :], s1_s.at[k])
    for t in range(2):
        landed(wbuf.at[pl.ds(t * 4, 4), 0], w_s.at[t])


def local(gate_pre, up_pre, out_grad, w_down, m_down, v_down):
    vmem = pl.BlockSpec(memory_space=pltpu.VMEM)
    hbm = pl.BlockSpec(memory_space=pl.ANY)
    dma = pltpu.SemaphoreType.DMA
    scratch = [
        pltpu.VMEM((8 * HB, TB), BF),
        pltpu.VMEM((8 * HB, TB), BF),
        pltpu.VMEM((2, HB, 16 * TB), BF),
        pltpu.VMEM((8, 2048, 256), BF),
        pltpu.VMEM((8, 2, HB, 256), BF),
        pltpu.VMEM((2, 3, 2, 2, HB, TILE), BF),
        pltpu.VMEM((2, 3, 2, 2, HB, TILE), BF),
        pltpu.VMEM((2, 2, 2, HB, TILE), F32),
        pltpu.VMEM((2, 3, HB, TILE), BF),
        pltpu.VMEM((2, 3, HB, TILE), BF),
        pltpu.VMEM((2, HB, TILE), F32),
        pltpu.VMEM((2, HB, 256), BF),
        pltpu.VMEM((4, 2, HB, 512), F32),
        pltpu.VMEM((4, 2, 2, HB, TB), BF),
        pltpu.VMEM((4, 2, 2, HB, TB), BF),
        pltpu.VMEM((4, 2, HB, TB), BF),
        pltpu.VMEM((4, 2, HB, TB), BF),
        pltpu.VMEM((3, 2, HB, TB), BF),
        pltpu.VMEM((4, 2, HB, TB), BF),
        dma((8,)), dma((8, 4)),
        dma((8, 2)), dma((8, 2)),
        dma((8, 2)), dma((8, 2)),
        dma((4, 2)), dma((4, 2)),
        dma((4, 2)), dma((4, 2)),
        dma((4,)), dma((4,)),
        dma((2,)), dma((2,)), dma,
        dma((2, 3)), dma((2, 3)),
        dma((2, 3)), dma((2, 3)),
        dma((2,)), dma((2,)), dma((2,)),
        dma((2, 4, 2)), dma((2, 4, 2)),
        dma((2, 4, 2)), dma((2, 4, 2)),
        dma((4,)), dma((4,)),
        dma((4,)), dma((4,)),
        dma((3,)), dma((3,)),
    ]
    dgu, dirs, first, second = pl.pallas_call(
        kernel,
        name="step",
        out_shape=(
            jax.ShapeDtypeStruct((2, TB, 8 * HB), BF),
            jax.ShapeDtypeStruct((HB, 16 * ROWS), BF),
            jax.ShapeDtypeStruct((HB, ROWS), F32),
            jax.ShapeDtypeStruct((HB, ROWS), F32),
        ),
        in_specs=[vmem, vmem, vmem, hbm, vmem, vmem],
        out_specs=(vmem, hbm, vmem, vmem),
        scratch_shapes=scratch,
        compiler_params=pltpu.CompilerParams(
            collective_id=0, has_side_effects=True, vmem_limit_bytes=60 << 20
        ),
        cost_estimate=pl.CostEstimate(flops=15 * 10**9, bytes_accessed=40 * 10**6, transcendentals=0),
    )(gate_pre, up_pre, out_grad, w_down.T, m_down.T, v_down.T)
    return (dgu.transpose(1, 0, 2), dirs.T, first.T, second.T)


def solution(mesh):
    return jax.shard_map(
        local,
        mesh=mesh,
        in_specs=(
            P(("replica", "shard"), None),
            P(("replica", "shard"), None),
            P(("replica", "shard"), None),
            P(None, "shard"),
            P("replica", "shard"),
            P("replica", "shard"),
        ),
        out_specs=(
            P(("replica", "shard"), None, None),
            P(None, "shard"),
            P("replica", "shard"),
            P("replica", "shard"),
        ),
        check_vma=False,
    )
```

time: 236 us -> 165 us (0.70)
  local copies, waits for them, and re-layouts: 57.3 us -> 13.6 us
  Pallas kernels: 176 us -> 150 us
    pallas_call x1, Pallas kernels: 176 us -> 150 us  [local(): pl.pallas_call(kernel, name='step', out_shape=(jax.ShapeDtypeStruct((2, T...]
    transpose x1 -> x0, local copies, waits for them, and re-layouts: 21.3 us -> none  [local(): direction = dirs.transpose(3, 2, 0, 4, 1, 5, 6).reshape(16 * ROWS, HB)]
    reshape x1 -> x0, local copies, waits for them, and re-layouts: 12.9 us -> none  [local(): direction = dirs.transpose(3, 2, 0, 4, 1, 5, 6).reshape(16 * ROWS, HB)]
    unnamed x10 -> x8, local copies, waits for them, and re-layouts: 23.1 us -> 13.6 us
where the time goes in v2:
time: 165 us
  Pallas kernels  150 us (91%)
  local copies, waits for them, and re-layouts  13.6 us (8%)
    pallas_call x1, Pallas kernels, local(): pl.pallas_call(kernel, name='step', out_shape=(jax.ShapeDtypeStruct((2, T...  150 us
    unnamed x8, local copies, waits for them, and re-layouts  13.6 us

profile of v2, /device:TPU:1, one launch (start us, length us, event | category | flops | bytes accessed | tf_op | source)
XLA Modules:
  0.0 164.5 jit_solution(15830414481472364788)
XLA Ops:
  0.6 150.3 %step.1 = (bf16[2,128,3584]{2,1,0:T(8,128)(2,1)}, bf16[448,8192]{1,0:T(8,128)(2,1)}, f32[448,512]{1,0:T(8,128)}, f32[448,512]{1,0:T(8,128)}) custom-call(bf16[128,3584]{1,0:T(8,128)(2,1)} %gate.1, bf16[128,3584]{1,0:T(8,128)(2,1)} %up.1, bf16[128,8192]{1,0:T(8,128)(2,1)} %og.1, bf16[448,8192]{1,0:T(8,128)(2,1)} %bitcast.11, f32[448,512]{1,0:T(8,128)} %bitcast.12, ...), custom_call_target="tpu_custom_call" | custom-call | flops 15000000512 | bytes 40000000 | tf_op jit(solution)/shard_map/step/pallas_call | solution.py:424
  151.0 4.6 %copy.10 = bf16[128,2,3584]{2,1,0:T(2,128)(2,1)} copy(bf16[128,2,3584]{2,0,1:T(8,128)(2,1)} %bitcast.8) | data formatting | bytes 3670016
  155.6 0.0 copy-start.1
  155.6 0.0 copy-start
  155.6 7.1 %copy.14 = bf16[8192,448]{0,1:T(8,128)(2,1)} copy(bf16[8192,448]{0,1:T(8,128)(2,1)} %bitcast.7) | data formatting | bytes 14680064
  162.7 0.0 copy-done.1
  162.7 0.9 copy.15
  163.6 0.0 copy-done
  163.6 0.9 copy.16
Async XLA Ops:
  155.6 7.1 %copy-start.1 = (f32[448,512]{1,0:T(8,128)S(1)}, f32[448,512]{1,0:T(8,128)}, u32[]{:S(2)}) copy-start(f32[448,512]{1,0:T(8,128)} %get-tuple-element.10) | copy-start | bytes 2752516
  155.6 8.0 %copy-start = (f32[448,512]{1,0:T(8,128)S(1)}, f32[448,512]{1,0:T(8,128)}, u32[]{:S(2)}) copy-start(f32[448,512]{1,0:T(8,128)} %get-tuple-element.11) | copy-start | bytes 2752516

commit v3 on v2

--- a/solution.py
+++ b/solution.py
@@ -32,7 +32,7 @@
     hid_own, d_own, hid, ogb, wbuf, rs_send, rs_recv, own, zs_send, zs_recv, gk, dir_own,
     dk, cs_send, cs_recv, zd_send, zd_recv, yd_send, yd_recv,
     s1_s, s1_r, s2_s, s2_r, fw_s, fw_r, h1_s, h1_r, h2_s, h2_r, h3_s, h3_r, w_s, w_r, w_l,
-    rs_s, rs_r, zs_s, zs_r, a_l, a_s, a_r, b_s, b_r, c_s, c_r,
+    rs_s, rs_r, zs_s, zs_r, a_l, a_s, a_r, b_s, b_r, f_s, f_r, c_s, c_r,
     cs_s, cs_r, zd_s, zd_r, yd_s, yd_r,
 ):
     rep, sh = lax.axis_index("replica"), lax.axis_index("shard")
@@ -183,9 +183,9 @@
             push(zs_send.at[t, n], zs_recv.at[t, n], zs_s.at[t, n], zs_r.at[t, n], to)
         gk[t] = total(zh, zl)
 
-    def block(zh2, x2, c2, t):
+    def block(zh2, x2, c2, t, lo=0, size=HB):
         r = zh2 * 8 + x2 * 2 + c2
-        return dirs.at[:, pl.ds(pl.multiple_of(r * ROWS + t * 256, 256), 256)]
+        return dirs.at[pl.ds(lo, size), pl.ds(pl.multiple_of(r * ROWS + t * 256, 256), 256)]
 
     def adam(t):
         for n in range(3):
@@ -203,7 +203,7 @@
             dir_own[t, :, pl.ds(pl.multiple_of(half * TILE, TILE), TILE)] = direction.astype(BF)
         place, src = block(zh, x, c, t), dir_own.at[t]
         push(src, place, a_s.at[t], a_r.at[t], dev(dzh=1))
-        for j in (2, 1, 3):
+        for j in (1, 3):
             push(src, place, b_s.at[t, j, 0], b_r.at[t, j, 0], dev(dx=j))
         push(src, place, c_s.at[t, 0, 0], c_r.at[t, 0, 0], dev(dc=1))
         pltpu.make_async_copy(src, place, a_l.at[t]).start()
@@ -211,15 +211,25 @@
     def dir_x(t):
         blk = block(1 - zh, x, c, t)
         landed(blk, a_r.at[t])
-        for j in (2, 1, 3):
+        for j in (1, 3):
             push(blk, blk, b_s.at[t, j, 1], b_r.at[t, j, 1], dev(dx=j))
         push(blk, blk, c_s.at[t, 0, 1], c_r.at[t, 0, 1], dev(dc=1))
 
-    def dir_core(t, n):
-        for j in (1, 3, 2):
-            blk = block(zh if n == 0 else 1 - zh, (x - j) % 4, c, t)
+    def dir_fw(t, n):
+        z = zh if n == 0 else 1 - zh
+        for j, lo in ((1, 0), (3, HB // 2)):
+            blk = block(z, (x - j) % 4, c, t)
             landed(blk, b_r.at[t, j, n])
+            part = block(z, (x - j) % 4, c, t, lo, HB // 2)
+            push(part, part, f_s.at[t, j, n], f_r.at[t, j, n], dev(dx=j))
             push(blk, blk, c_s.at[t, j, n], c_r.at[t, j, n], dev(dc=1))
+
+    def dir_far(t, n):
+        z, far = zh if n == 0 else 1 - zh, (x + 2) % 4
+        for j, lo in ((1, 0), (3, HB // 2)):
+            landed(block(z, far, c, t, lo, HB // 2), f_r.at[t, j, n])
+        blk = block(z, far, c, t)
+        push(blk, blk, c_s.at[t, 2, n], c_r.at[t, 2, n], dev(dc=1))
 
     def dir_end(t):
         landed(block(zh, x, c, t), a_l.at[t])
@@ -301,30 +311,31 @@
     quarter(0)
     hid_z(0)
     quarter(1)
+    spread(0)
+    hid_z(1)
+    hid_z(2)
     quarter(2)
-    spread(0)
     spread(1)
-    hid_z(1)
-    quarter(3)
-    hid_z(2)
-    quarter(4)
     hid_core(0)
     hid_z(3)
-    for k in (5, 6, 7):
-        quarter(k)
+    quarter(3)
+    quarter(4)
+    hid_core(1)
+    quarter(5)
+    quarter(6)
+    quarter(7)
     forward(0)
     spread(2)
-    hid_core(1)
+    hid_core(2)
     forward(1)
+    hid_core(3)
     spread(3)
-    hid_core(2)
-    forward(2)
-    spread(4)
-    hid_core(3)
-    weights()
     for n in range(4):
         hid_end(n)
     grad(0)
+    weights()
+    forward(2)
+    spread(4)
     grad(1)
     forward(3)
     spread(5)
@@ -332,44 +343,48 @@
     forward(4)
     spread(6)
     grad(3)
+    x_sum(0)
+    forward(5)
+    spread(7)
+    grad(4)
+    adam(0)
     landed(wbuf.at[:, zl], w_l)
     landed(wbuf.at[pl.ds(0, 4), 1 - zl], w_r.at[0])
     dh_early(0)
-    forward(5)
-    spread(7)
-    grad(4)
-    x_sum(0)
+    forward(6)
+    dir_x(0)
+    grad(5)
     dh_early(1)
-    forward(6)
-    grad(5)
-    adam(0)
     dh_early(2)
     forward(7)
     grad(6)
-    dir_x(0)
+    dir_fw(0, 0)
     dh_early(3)
     grad(7)
     landed(wbuf.at[pl.ds(4, 4), 1 - zl], w_r.at[1])
     dh_late(0)
-    x_sum(1)
     dh_late(1)
     dh_core(0)
+    x_sum(1)
+    dir_fw(0, 1)
     dh_late(2)
+    dh_late(3)
+    dir_far(0, 0)
+    adam(1)
     dh_core(1)
-    adam(1)
-    dh_late(3)
     dh_z(0)
+    dir_far(0, 1)
     dh_core(2)
     dir_x(1)
-    dir_core(0, 0)
-    dir_core(0, 1)
+    dir_fw(1, 0)
     dh_z(1)
     dh_core(3)
+    dir_fw(1, 1)
     dh_z(2)
+    dir_far(1, 0)
+    dir_far(1, 1)
     dh_z(3)
-    dir_core(1, 0)
     cotangents()
-    dir_core(1, 1)
     dir_end(0)
     dir_end(1)
 
@@ -417,6 +432,7 @@
         dma((2,)), dma((2,)), dma((2,)),
         dma((2, 4, 2)), dma((2, 4, 2)),
         dma((2, 4, 2)), dma((2, 4, 2)),
+        dma((2, 4, 2)), dma((2, 4, 2)),
         dma((4,)), dma((4,)),
         dma((4,)), dma((4,)),
         dma((3,)), dma((3,)),

time: 165 us -> 155 us (0.939)
  Pallas kernels: 150 us -> 140 us
    pallas_call x1, Pallas kernels: 150 us -> 140 us  [local(): pl.pallas_call(kernel, name='step', out_shape=(jax.ShapeDtypeStruct((2, T...]
where the time goes in v3:
time: 155 us
  Pallas kernels  140 us (90%)
  local copies, waits for them, and re-layouts  13.6 us (9%)
    pallas_call x1, Pallas kernels, local(): pl.pallas_call(kernel, name='step', out_shape=(jax.ShapeDtypeStruct((2, T...  140 us
    unnamed x8, local copies, waits for them, and re-layouts  13.6 us

profile of v3, /device:TPU:1, one launch (start us, length us, event | category | flops | bytes accessed | tf_op | source)
XLA Modules:
  0.0 154.6 jit_solution(17728345048777845797)
XLA Ops:
  0.6 140.4 %step.1 = (bf16[2,128,3584]{2,1,0:T(8,128)(2,1)}, bf16[448,8192]{1,0:T(8,128)(2,1)}, f32[448,512]{1,0:T(8,128)}, f32[448,512]{1,0:T(8,128)}) custom-call(bf16[128,3584]{1,0:T(8,128)(2,1)} %gate.1, bf16[128,3584]{1,0:T(8,128)(2,1)} %up.1, bf16[128,8192]{1,0:T(8,128)(2,1)} %og.1, bf16[448,8192]{1,0:T(8,128)(2,1)} %bitcast.11, f32[448,512]{1,0:T(8,128)} %bitcast.12, ...), custom_call_target="tpu_custom_call" | custom-call | flops 15000000512 | bytes 40000000 | tf_op jit(solution)/shard_map/step/pallas_call | solution.py:440
  141.0 4.6 %copy.10 = bf16[128,2,3584]{2,1,0:T(2,128)(2,1)} copy(bf16[128,2,3584]{2,0,1:T(8,128)(2,1)} %bitcast.8) | data formatting | bytes 3670016
  145.6 0.0 copy-start.1
  145.6 0.0 copy-start
  145.7 7.1 %copy.14 = bf16[8192,448]{0,1:T(8,128)(2,1)} copy(bf16[8192,448]{0,1:T(8,128)(2,1)} %bitcast.7) | data formatting | bytes 14680064
  152.8 0.0 copy-done.1
  152.8 0.9 copy.15
  153.7 0.0 copy-done
  153.7 0.9 copy.16
Async XLA Ops:
  145.6 7.1 %copy-start.1 = (f32[448,512]{1,0:T(8,128)S(1)}, f32[448,512]{1,0:T(8,128)}, u32[]{:S(2)}) copy-start(f32[448,512]{1,0:T(8,128)} %get-tuple-element.10) | copy-start | bytes 2752516
  145.6 8.0 %copy-start = (f32[448,512]{1,0:T(8,128)S(1)}, f32[448,512]{1,0:T(8,128)}, u32[]{:S(2)}) copy-start(f32[448,512]{1,0:T(8,128)} %get-tuple-element.11) | copy-start | bytes 2752516

commit v4 on v3

--- a/solution.py
+++ b/solution.py
@@ -21,9 +21,9 @@
 HB = 448
 ROWS = 512
 TILE = 128
-X_ORDER = (2, 1, 3, 0)
+PAIRS = (((0, 2), (1, 2)), ((0, 1), (0, 3)), ((1, 1), (1, 3)), ((0, 0), (1, 0)))
 Y_ORDER = (2, 1, 3, 0)
-STEPS = [(t, j) for t in range(2) for j in X_ORDER]
+STEPS = [(t, pair) for t in range(2) for pair in PAIRS]
 
 
 def kernel(
@@ -114,11 +114,11 @@
         landed(hid.at[:, :, tok(ys, (1 - zl) * 2 + 1 - c)], h3_r.at[n])
 
     def quarter(k):
-        t, j = STEPS[k]
+        t, pair = STEPS[k]
         for dzl, dc in ((1, 0), (1, 1), (0, 1), (0, 0)):
-            for z in range(2):
+            for p, (z, j) in enumerate(pair):
                 cols = pl.ds(d_row(z, j, (c + dc) % 2, (zl + dzl) % 2, t), TILE)
-                dst = ogb.at[k, tok(y, q), pl.ds(z * TILE, TILE)]
+                dst = ogb.at[k, tok(y, q), pl.ds(p * TILE, TILE)]
                 if dzl or dc:
                     push(og.at[:, cols], dst, s1_s.at[k], s1_r.at[k, q], dev(dc=dc, dzl=dzl), keep=False)
                 else:
@@ -131,9 +131,9 @@
             push(ogb.at[k, slot(y), :], ogb.at[k, slot(y), :], s2_s.at[k, n], s2_r.at[k, n], dev(dy=dy))
 
     def weights():
-        for k, (t, j) in enumerate(STEPS):
-            for z in range(2):
-                half = pl.ds(z * TILE, TILE)
+        for k, (t, pair) in enumerate(STEPS):
+            for p, (z, j) in enumerate(pair):
+                half = pl.ds(p * TILE, TILE)
                 mine = pl.ds(d_row(z, j, c, zl, t), TILE)
                 theirs = pl.ds(d_row(z, j, c, 1 - zl, t), TILE)
                 pltpu.make_async_copy(w.at[:, mine], wbuf.at[k, zl, :, half], w_l).start()
@@ -149,7 +149,7 @@
         push(part, part, fw_s.at[k, 1], fw_r.at[k, 1], dev(dy=3))
 
     def grad(k):
-        t, j = STEPS[k]
+        t, pair = STEPS[k]
         far = (y + 2) % 4
         landed(ogb.at[k, slot(far, 0, 256), :], fw_r.at[k, 0])
         landed(ogb.at[k, slot(far, 256, 256), :], fw_r.at[k, 1])
@@ -157,19 +157,22 @@
         @pl.loop(0, 2)
         def _(b):
             prod = jnp.dot(hid[b], ogb[k], preferred_element_type=F32)
-            for z in range(2):
-                part = prod[:, z * TILE : (z + 1) * TILE]
+            for p, (z, j) in enumerate(pair):
+                part = prod[:, p * TILE : (p + 1) * TILE]
                 if j:
                     rs_send[t, j - 1, z, b] = part.astype(BF)
                 else:
                     own[t, z, b] = part
 
-        if j:
-            push(rs_send.at[t, j - 1], rs_recv.at[t, j - 1], rs_s.at[t, j - 1], rs_r.at[t, j - 1], dev(dx=j))
+        for z, j in pair:
+            if j:
+                at = (t, j - 1, z)
+                push(rs_send.at[at], rs_recv.at[at], rs_s.at[at], rs_r.at[at], dev(dx=j))
 
     def x_sum(t):
         for j in (1, 2, 3):
-            landed(rs_recv.at[t, j - 1], rs_r.at[t, j - 1])
+            for z in range(2):
+                landed(rs_recv.at[t, j - 1, z], rs_r.at[t, j - 1, z])
 
         def total(z, b):
             out = own[t, z, b]
@@ -427,7 +430,7 @@
         dma((4, 2)), dma((4, 2)),
         dma((4,)), dma((4,)),
         dma((2,)), dma((2,)), dma,
-        dma((2, 3)), dma((2, 3)),
+        dma((2, 3, 2)), dma((2, 3, 2)),
         dma((2, 3)), dma((2, 3)),
         dma((2,)), dma((2,)), dma((2,)),
         dma((2, 4, 2)), dma((2, 4, 2)),

time: 155 us -> 155 us (level)
  no operation moved by 1% of the time
where the time goes in v4:
time: 155 us
  Pallas kernels  141 us (91%)
  local copies, waits for them, and re-layouts  13.6 us (9%)
    pallas_call x1, Pallas kernels, local(): pl.pallas_call(kernel, name='step', out_shape=(jax.ShapeDtypeStruct((2, T...  141 us
    unnamed x8, local copies, waits for them, and re-layouts  13.6 us

profile of v4, /device:TPU:1, one launch (start us, length us, event | category | flops | bytes accessed | tf_op | source)
XLA Modules:
  0.0 154.7 jit_solution(13507010907691630321)
XLA Ops:
  0.6 140.5 %step.1 = (bf16[2,128,3584]{2,1,0:T(8,128)(2,1)}, bf16[448,8192]{1,0:T(8,128)(2,1)}, f32[448,512]{1,0:T(8,128)}, f32[448,512]{1,0:T(8,128)}) custom-call(bf16[128,3584]{1,0:T(8,128)(2,1)} %gate.1, bf16[128,3584]{1,0:T(8,128)(2,1)} %up.1, bf16[128,8192]{1,0:T(8,128)(2,1)} %og.1, bf16[448,8192]{1,0:T(8,128)(2,1)} %bitcast.11, f32[448,512]{1,0:T(8,128)} %bitcast.12, ...), custom_call_target="tpu_custom_call" | custom-call | flops 15000000512 | bytes 40000000 | tf_op jit(solution)/shard_map/step/pallas_call | solution.py:443
  141.1 4.6 %copy.10 = bf16[128,2,3584]{2,1,0:T(2,128)(2,1)} copy(bf16[128,2,3584]{2,0,1:T(8,128)(2,1)} %bitcast.8) | data formatting | bytes 3670016
  145.8 0.0 copy-start.1
  145.8 0.0 copy-start
  145.8 7.1 %copy.14 = bf16[8192,448]{0,1:T(8,128)(2,1)} copy(bf16[8192,448]{0,1:T(8,128)(2,1)} %bitcast.7) | data formatting | bytes 14680064
  152.9 0.0 copy-done.1
  152.9 0.9 copy.15
  153.8 0.0 copy-done
  153.8 0.9 copy.16
Async XLA Ops:
  145.8 7.1 %copy-start.1 = (f32[448,512]{1,0:T(8,128)S(1)}, f32[448,512]{1,0:T(8,128)}, u32[]{:S(2)}) copy-start(f32[448,512]{1,0:T(8,128)} %get-tuple-element.10) | copy-start | bytes 2752516
  145.8 8.0 %copy-start = (f32[448,512]{1,0:T(8,128)S(1)}, f32[448,512]{1,0:T(8,128)}, u32[]{:S(2)}) copy-start(f32[448,512]{1,0:T(8,128)} %get-tuple-element.11) | copy-start | bytes 2752516
